TPU v7x, 256 devices: a whole 4x4x8 slice. The times are simulated.
256 devices in a mesh: depth: 16 (over z, core), image: 16 (over x, y).
Axes of the slice: x: 4, y: 4, z: 8, core: 2. Of those that a mesh axis runs over, the one named last changes fastest.
Arguments:
- level_set: float32 [256, 1024, 512], P('depth', 'image'), may hold values from -6 to 6
- velocity: float32 [3, 256, 1024, 512], P(None, 'depth', 'image'), may hold values from -1 to 1
- view_flag: int32 [16], replicated, may hold values from 0 to 1
- slab_rank: int32 [16], replicated, may hold values from 0 to 15, each once
Outputs:
- image_first: float32 [4, 1024, 512], P(None, 'image', 'depth')
- image_second: float32 [4, 1024, 512], P(None, 'image', 'depth')
- level_next: float32 [256, 1024, 512], P('depth', 'image')
Inputs may be any that keep to these rules, and one draw needn't show every extreme that they name: `slab_rank`: each of 0 to 15 once.
All inputs are finite; a program needn't handle non-finite values.
Results may differ from a plain program's by a relative error of at most 0.00013.
Values sent between devices are 32-bit elements; how exact they have to be, the bound alone decides.
A program may use at most 64 MiB of HBM per device.

v0:
```python
import jax
import jax.numpy as jnp
from jax import lax
from jax.sharding import PartitionSpec as P

STEPS = 4
step_size = 0.3


def padded_2(array, sides, width):
    edges = {}
    for axis, dim in sides:
        size, length = (lax.axis_size(axis), array.shape[dim])
        up = [(i, (i + 1) % size) for i in range(size - 1)]
        last = lax.slice_in_dim(array, length - width, length, axis=dim)
        leading = lax.slice_in_dim(array, 0, width, axis=dim)
        edges[dim] = (
            lax.ppermute(last, axis, up),
            lax.ppermute(leading, axis, [(b, a) for a, b in up]),
        )
    done = []
    for _, dim in sides:
        low, high = edges[dim]
        around = [(width, width) if d in done else (0, 0) for d in range(array.ndim)]
        array = jnp.concatenate([jnp.pad(low, around), array, jnp.pad(high, around)], axis=dim)
        done.append(dim)
    return array


def update(padded, velocity):
    center = padded[1:-1, 1:-1, 1:-1]
    lows = (padded[:-2, 1:-1, 1:-1], padded[1:-1, :-2, 1:-1], padded[1:-1, 1:-1, :-2])
    highs = (padded[2:, 1:-1, 1:-1], padded[1:-1, 2:, 1:-1], padded[1:-1, 1:-1, 2:])
    rate = jnp.zeros_like(center)
    for k in range(3):
        speed = velocity[k]
        rate = (
            rate
            + jnp.maximum(speed, 0.0) * (center - lows[k])
            + jnp.minimum(speed, 0.0) * (highs[k] - center)
        )
    return center - step_size * rate


def advect_single(field, velocity):
    padded = padded_2(field, (("depth", 0), ("image", 1)), 1)
    padded = jnp.pad(padded, ((0, 0), (0, 0), (1, 1)))
    return update(padded, velocity)


def render_brick(field, flag, scale):
    density = scale * jnp.exp(-field * field)
    colour = jnp.stack(
        [jax.nn.sigmoid(2.0 * field), jnp.exp(-field * field), jax.nn.sigmoid(-2.0 * field)], axis=0
    )
    running = jnp.cumsum(density, axis=0)
    totals = running[-1:]
    before = jnp.where(flag[0] == 0, running - density, totals - running)
    weight = jnp.exp(-before) * (1.0 - jnp.exp(-density))
    partial_colour = jnp.sum(weight[None] * colour, axis=1)
    return (partial_colour, -totals[0])


def composite(frames, slab_rank):
    count = len(frames)
    depth_count = lax.axis_size("depth")
    colours = jnp.stack([frame[0] for frame in frames], axis=0)
    logs = jnp.stack([frame[1] for frame in frames], axis=0)
    rows, cols = (logs.shape[1], logs.shape[2])
    width = cols // depth_count
    packed = jnp.concatenate([colours, logs[:, None]], axis=1)
    received = lax.all_to_all(packed, "depth", split_axis=3, concat_axis=0, tiled=True)
    received = received.reshape(depth_count, count, 4, rows, width)
    earlier_mask = (slab_rank[None, :] < slab_rank[:, None]).astype(jnp.float32)
    log_parts = received[:, :, 3]
    earlier = jnp.einsum("de,efxy->dfxy", earlier_mask, log_parts, precision=lax.Precision.HIGHEST)
    rgb = jnp.sum(jnp.exp(earlier)[:, :, None] * received[:, :, :3], axis=0)
    alpha = 1.0 - jnp.exp(jnp.sum(log_parts, axis=0))
    result = jnp.concatenate([rgb, alpha[:, None]], axis=1)
    return [result[0]]


def local(level_set, velocity, view_flag, slab_rank):
    scale = 2.0 / (level_set.shape[0] * lax.axis_size("depth"))
    own_flag = lax.dynamic_slice_in_dim(view_flag, lax.axis_index("depth"), 1)
    first = render_brick(level_set, own_flag, scale)
    field = level_set
    for step in range(STEPS):
        field = advect_single(field, velocity)
    second = render_brick(field, own_flag, scale)
    image_first = composite([first], slab_rank)[0]
    image_second = composite([second], slab_rank)[0]
    return (image_first, image_second, field)


def solution(mesh):
    placed = (P("depth", "image", None), P(None, "depth", "image", None), P(), P())
    return jax.shard_map(
        local,
        mesh=mesh,
        in_specs=placed,
        out_specs=(P(None, "image", "depth"), P(None, "image", "depth"), P("depth", "image", None)),
        check_vma=False,
    )
```

profile of v0, /device:TPU:27, one launch (start us, length us, event | category | flops | bytes accessed | tf_op | source)
XLA Modules:
  0.0 151.2 jit_solution(3199686916753563401)
XLA Ops:
  1.7 2.4 %collective-permute-start.3 = (f32[16,1,512]{2,1,0:T(1,128)S(1)}, f32[16,1,512]{2,1,0:T(1,128)S(1)}, u32[]{:S(2)}, u32[]{:S(2)}) collective-permute-start(f32[16,1,512]{2,1,0:T(1,128)S(1)} %get-tuple-element.28), channel_id=1, source_target_pairs={{1,0},{2,1},{3,2},{4,3},{5,4},{6,5},{7,6},{8,7},{9,8},{10,9},{11,1... | collective-permute-start | bytes 98312 | tf_op jit(solution)/shard_map/ppermute | solution.py:19
  5.1 4.4 %collective-permute-start = (f32[1,64,512]{2,1,0:T(8,128)S(1)}, f32[1,64,512]{2,1,0:T(8,128)S(1)}, u32[]{:S(2)}, u32[]{:S(2)}) collective-permute-start(f32[1,64,512]{2,1,0:T(8,128)S(1)} %get-tuple-element.30), channel_id=1, source_target_pairs={{0,16},{16,32},{32,48},{48,64},{64,80},{80,96},{96,112},{112,128},... | collective-permute-start | bytes 393224 | tf_op jit(solution)/shard_map/ppermute | solution.py:18
  9.5 1.9 %collective-permute-start.1 = (f32[1,64,512]{2,1,0:T(8,128)S(1)}, f32[1,64,512]{2,1,0:T(8,128)S(1)}, u32[]{:S(2)}, u32[]{:S(2)}) collective-permute-start(f32[1,64,512]{2,1,0:T(8,128)S(1)} %get-tuple-element.29), channel_id=1, source_target_pairs={{16,0},{32,16},{48,32},{64,48},{80,64},{96,80},{112,96},{128,112},... | collective-permute-start | bytes 393224 | tf_op jit(solution)/shard_map/ppermute | solution.py:19
  11.4 5.0 %collective-permute-start.2 = (f32[16,1,512]{2,1,0:T(1,128)S(1)}, f32[16,1,512]{2,1,0:T(1,128)S(1)}, u32[]{:S(2)}, u32[]{:S(2)}) collective-permute-start(f32[16,1,512]{2,1,0:T(1,128)S(1)} %get-tuple-element.27), channel_id=1, source_target_pairs={{0,1},{1,2},{2,3},{3,4},{4,5},{5,6},{6,7},{7,8},{8,9},{9,10},{10,1... | collective-permute-start | bytes 98312 | tf_op jit(solution)/shard_map/ppermute | solution.py:18
  16.5 2.2 %fusion.75 = f32[16,64,512]{2,1,0:T(8,128)S(1)} fusion(f32[16,64,512]{2,1,0:T(8,128)} %param.4), kind=kOutput, calls=%fused_computation.143 | output fusion | flops 9437184 | bytes 4194304 | tf_op jit(solution)/shard_map/jit(cumsum)/reduce_window_sum | solution.py:56
  25.7 6.7 %fusion.59 = (f32[16,64,512]{2,1,0:T(8,128)S(1)}, f32[1,16,64,512]{3,2,1,0:T(8,128)}, f32[16,64,512]{2,1,0:T(8,128)}, f32[1,16,64,512]{3,2,1,0:T(8,128)}, f32[1,16,64,512]{3,2,1,0:T(8,128)}) fusion(f32[16,64,512]{2,1,0:T(8,128)S(1)} %copy-done, f32[18,66,514]{2,1,0:T(8,128)S(1)} %select_maximum_fusion.12, f32[18,1,512]{2,1,0:T(1,128)S(1)} %pad.39, ...), kind=kLoop, calls=%fused_computation.110 | loop fusion | flops 24641536 | bytes 27992064 | tf_op jit(solution)/shard_map/sub | solution.py:42
  32.4 1.9 %collective-permute-start.5 = (f32[1,64,512]{2,1,0:T(8,128)S(1)}, f32[1,64,512]{2,1,0:T(8,128)S(1)}, u32[]{:S(2)}, u32[]{:S(2)}) collective-permute-start(f32[1,64,512]{2,1,0:T(8,128)S(1)} %get-tuple-element.19), channel_id=1, source_target_pairs={{16,0},{32,16},{48,32},{64,48},{80,64},{96,80},{112,96},{128,112},... | collective-permute-start | bytes 393224 | tf_op jit(solution)/shard_map/ppermute | solution.py:19
  34.4 3.9 %collective-permute-start.4 = (f32[1,64,512]{2,1,0:T(8,128)S(1)}, f32[1,64,512]{2,1,0:T(8,128)S(1)}, u32[]{:S(2)}, u32[]{:S(2)}) collective-permute-start(f32[1,64,512]{2,1,0:T(8,128)S(1)} %get-tuple-element.18), channel_id=1, source_target_pairs={{0,16},{16,32},{32,48},{48,64},{64,80},{80,96},{96,112},{112,128},... | collective-permute-start | bytes 393224 | tf_op jit(solution)/shard_map/ppermute | solution.py:18
  40.3 5.5 %collective-permute-start.6 = (f32[16,1,512]{2,1,0:T(1,128)S(1)}, f32[16,1,512]{2,1,0:T(1,128)S(1)}, u32[]{:S(2)}, u32[]{:S(2)}) collective-permute-start(f32[16,1,512]{2,1,0:T(1,128)S(1)} %get-tuple-element.20), channel_id=1, source_target_pairs={{0,1},{1,2},{2,3},{3,4},{4,5},{5,6},{6,7},{7,8},{8,9},{9,10},{10,1... | collective-permute-start | bytes 98312 | tf_op jit(solution)/shard_map/ppermute | solution.py:18
  46.8 3.0 %select_maximum_fusion.8 = f32[18,66,514]{2,1,0:T(8,128)S(1)} fusion(f32[18,1,512]{2,1,0:T(1,128)S(1)} %pad.42, f32[18,1,512]{2,1,0:T(1,128)S(1)} %pad.41, f32[1,64,512]{2,1,0:T(8,128)S(1)} %collective-permute-done.5, f32[16,64,512]{2,1,0:T(8,128)S(1)} %get-tuple-element.22, f32[1,64,512]{2,1,0:T(8,128)S(1)} %collective-permute-done.4), kind=kLoop, calls=%fused_computation.14 | loop fusion | flops 7327584 | bytes 4875552 | tf_op jit(solution)/shard_map/concatenate | solution.py:25
  49.9 3.5 %fusion.42 = f32[16,64,512]{2,1,0:T(8,128)S(1)} fusion(f32[16,64,512]{2,1,0:T(8,128)S(1)} %get-tuple-element.22, f32[18,66,514]{2,1,0:T(8,128)S(1)} %select_maximum_fusion.8, f32[18,1,512]{2,1,0:T(1,128)S(1)} %pad.42, f32[1,64,512]{2,1,0:T(8,128)S(1)} %collective-permute-done.5, f32[1,64,512]{2,1,0:T(8,128)S(1)} %collective-permute-done.4, ...), kind=kLoop, calls=%fused_computation.83 | loop fusion | flops 17301504 | bytes 15015936 | tf_op jit(solution)/shard_map/sub | solution.py:42
  53.5 1.9 %collective-permute-start.11 = (f32[16,1,512]{2,1,0:T(1,128)S(1)}, f32[16,1,512]{2,1,0:T(1,128)S(1)}, u32[]{:S(2)}, u32[]{:S(2)}) collective-permute-start(f32[16,1,512]{2,1,0:T(1,128)S(1)} %get-tuple-element.17), channel_id=1, source_target_pairs={{1,0},{2,1},{3,2},{4,3},{5,4},{6,5},{7,6},{8,7},{9,8},{10,9},{11,1... | collective-permute-start | bytes 98312 | tf_op jit(solution)/shard_map/ppermute | solution.py:19
  55.4 5.8 %collective-permute-start.10 = (f32[16,1,512]{2,1,0:T(1,128)S(1)}, f32[16,1,512]{2,1,0:T(1,128)S(1)}, u32[]{:S(2)}, u32[]{:S(2)}) collective-permute-start(f32[16,1,512]{2,1,0:T(1,128)S(1)} %get-tuple-element.16), channel_id=1, source_target_pairs={{0,1},{1,2},{2,3},{3,4},{4,5},{5,6},{6,7},{7,8},{8,9},{9,10},{10,1... | collective-permute-start | bytes 98312 | tf_op jit(solution)/shard_map/ppermute | solution.py:18
  61.1 2.1 %collective-permute-start.9 = (f32[1,64,512]{2,1,0:T(8,128)S(1)}, f32[1,64,512]{2,1,0:T(8,128)S(1)}, u32[]{:S(2)}, u32[]{:S(2)}) collective-permute-start(f32[1,64,512]{2,1,0:T(8,128)S(1)} %get-tuple-element.15), channel_id=1, source_target_pairs={{16,0},{32,16},{48,32},{64,48},{80,64},{96,80},{112,96},{128,112},... | collective-permute-start | bytes 393224 | tf_op jit(solution)/shard_map/ppermute | solution.py:19
  63.3 4.2 %collective-permute-start.8 = (f32[1,64,512]{2,1,0:T(8,128)S(1)}, f32[1,64,512]{2,1,0:T(8,128)S(1)}, u32[]{:S(2)}, u32[]{:S(2)}) collective-permute-start(f32[1,64,512]{2,1,0:T(8,128)S(1)} %get-tuple-element.14), channel_id=1, source_target_pairs={{0,16},{16,32},{32,48},{48,64},{64,80},{80,96},{96,112},{112,128},... | collective-permute-start | bytes 393224 | tf_op jit(solution)/shard_map/ppermute | solution.py:18
  69.2 3.0 %select_maximum_fusion.4 = f32[18,66,514]{2,1,0:T(8,128)S(1)} fusion(f32[18,1,512]{2,1,0:T(1,128)S(1)} %pad.45, f32[18,1,512]{2,1,0:T(1,128)S(1)} %pad.44, f32[1,64,512]{2,1,0:T(8,128)S(1)} %collective-permute-done.9, f32[16,64,512]{2,1,0:T(8,128)S(1)} %fusion.42, f32[1,64,512]{2,1,0:T(8,128)S(1)} %collective-permute-done.8), kind=kLoop, calls=%fused_computation.10 | loop fusion | flops 7327584 | bytes 4875552 | tf_op jit(solution)/shard_map/concatenate | solution.py:25
  72.2 3.5 %fusion.25 = f32[16,64,512]{2,1,0:T(8,128)S(1)} fusion(f32[16,64,512]{2,1,0:T(8,128)S(1)} %fusion.42, f32[18,66,514]{2,1,0:T(8,128)S(1)} %select_maximum_fusion.4, f32[18,1,512]{2,1,0:T(1,128)S(1)} %pad.45, f32[1,64,512]{2,1,0:T(8,128)S(1)} %collective-permute-done.9, f32[1,64,512]{2,1,0:T(8,128)S(1)} %collective-permute-done.8, f32[18,1,512]{2,1,0:T(1,128)S(1)} %pad.44, ...), kind=kLoop, calls=%fused_computation.56 | loop fusion | flops 17301504 | bytes 15015936 | tf_op jit(solution)/shard_map/sub | solution.py:42
  78.3 4.4 %collective-permute-start.12 = (f32[1,64,512]{2,1,0:T(8,128)S(1)}, f32[1,64,512]{2,1,0:T(8,128)S(1)}, u32[]{:S(2)}, u32[]{:S(2)}) collective-permute-start(f32[1,64,512]{2,1,0:T(8,128)S(1)} %get-tuple-element.10), channel_id=1, source_target_pairs={{0,16},{16,32},{32,48},{48,64},{64,80},{80,96},{96,112},{112,128},... | collective-permute-start | bytes 393224 | tf_op jit(solution)/shard_map/ppermute | solution.py:18
  85.3 5.5 %collective-permute-start.14 = (f32[16,1,512]{2,1,0:T(1,128)}, f32[16,1,512]{2,1,0:T(1,128)}, u32[]{:S(2)}, u32[]{:S(2)}) collective-permute-start(f32[16,1,512]{2,1,0:T(1,128)} %get-tuple-element.12), channel_id=1, source_target_pairs={{0,1},{1,2},{2,3},{3,4},{4,5},{5,6},{6,7},{7,8},{8,9},{9,10},{10,1... | collective-permute-start | bytes 98312 | tf_op jit(solution)/shard_map/ppermute | solution.py:18
  95.0 11.1 %all-to-all-start = ((f32[16,1,8192]{2,1,0:T(1,128)}), f32[16,1,8192]{2,1,0:T(1,128)S(1)}, u32[]{:S(2)}, u32[]{:S(2)}) async-start(f32[16,1,8192]{2,1,0:T(1,128)} %reshape.111), calls=%async_computation | async-start | bytes 1048576 | tf_op jit(solution)/shard_map/all_to_all | solution.py:72
  107.7 3.0 %select_maximum_fusion = f32[18,66,514]{2,1,0:T(8,128)S(1)} fusion(f32[18,1,512]{2,1,0:T(1,128)S(1)} %pad.48, f32[18,1,512]{2,1,0:T(1,128)S(1)} %pad.47, f32[1,64,512]{2,1,0:T(8,128)S(1)} %collective-permute-done.13, f32[16,64,512]{2,1,0:T(8,128)S(1)} %copy-done.2, f32[1,64,512]{2,1,0:T(8,128)S(1)} %collective-permute-done.12), kind=kLoop, calls=%fused_computation.6 | loop fusion | flops 7327584 | bytes 4875552 | tf_op jit(solution)/shard_map/concatenate | solution.py:25
  110.7 5.5 %divide_bitcast_fusion.1 = (f32[1,16,64,512]{3,2,1,0:T(8,128)S(1)}, f32[16,64,512]{2,1,0:T(8,128)S(1)}) fusion(f32[16,64,512]{2,1,0:T(8,128)S(1)} %copy-done.2, f32[18,66,514]{2,1,0:T(8,128)S(1)} %select_maximum_fusion, f32[3,16,64,512]{3,2,1,0:T(8,128)} %param.5, f32[18,1,512]{2,1,0:T(1,128)S(1)} %pad.48, f32[1,64,512]{2,1,0:T(8,128)S(1)} %collective-permute-done.13, ...), kind=kLoop, calls=%fused_computation.130 | loop fusion | flops 19398656 | bytes 17113088 | tf_op jit(solution)/shard_map/stack | solution.py:53
  123.4 6.0 %all-to-all-start.1 = ((f32[16,1,8192]{2,1,0:T(1,128)}), f32[16,1,8192]{2,1,0:T(1,128)S(1)}, u32[]{:S(2)}, u32[]{:S(2)}) async-start(f32[16,1,8192]{2,1,0:T(1,128)} %reshape.113), calls=%async_computation.1 | async-start | bytes 1048576 | tf_op jit(solution)/shard_map/all_to_all | solution.py:72
  134.4 12.4 %all-to-all-done.1 = f32[16,1,8192]{2,1,0:T(1,128)S(1)} async-done(((f32[16,1,8192]{2,1,0:T(1,128)}), f32[16,1,8192]{2,1,0:T(1,128)S(1)}, u32[]{:S(2)}, u32[]{:S(2)}) %all-to-all-start.1) | async-done | bytes 524320 | tf_op jit(solution)/shard_map/all_to_all | solution.py:72
  (99 shorter events, 40.6 us)
Async XLA Ops:
  1.7 19.5 %collective-permute-start.3 = (f32[16,1,512]{2,1,0:T(1,128)S(1)}, f32[16,1,512]{2,1,0:T(1,128)S(1)}, u32[]{:S(2)}, u32[]{:S(2)}) collective-permute-start(f32[16,1,512]{2,1,0:T(1,128)S(1)} %get-tuple-element.28), channel_id=1, source_target_pairs={{1,0},{2,1},{3,2},{4,3},{5,4},{6,5},{7,6},{8,7},{9,8},{10,9},{11,1... | collective-permute-start | bytes 98312 | tf_op jit(solution)/shard_map/ppermute | solution.py:19
  5.1 16.2 %collective-permute-start = (f32[1,64,512]{2,1,0:T(8,128)S(1)}, f32[1,64,512]{2,1,0:T(8,128)S(1)}, u32[]{:S(2)}, u32[]{:S(2)}) collective-permute-start(f32[1,64,512]{2,1,0:T(8,128)S(1)} %get-tuple-element.30), channel_id=1, source_target_pairs={{0,16},{16,32},{32,48},{48,64},{64,80},{80,96},{96,112},{112,128},... | collective-permute-start | bytes 393224 | tf_op jit(solution)/shard_map/ppermute | solution.py:18
  9.5 13.8 %collective-permute-start.1 = (f32[1,64,512]{2,1,0:T(8,128)S(1)}, f32[1,64,512]{2,1,0:T(8,128)S(1)}, u32[]{:S(2)}, u32[]{:S(2)}) collective-permute-start(f32[1,64,512]{2,1,0:T(8,128)S(1)} %get-tuple-element.29), channel_id=1, source_target_pairs={{16,0},{32,16},{48,32},{64,48},{80,64},{96,80},{112,96},{128,112},... | collective-permute-start | bytes 393224 | tf_op jit(solution)/shard_map/ppermute | solution.py:19
  11.4 8.6 %copy-start.11 = (s32[16]{0:T(128)S(1)}, s32[16]{0:T(128)}, u32[]{:S(2)}) copy-start(s32[16]{0:T(128)} %param.6) | copy-start | bytes 196
  11.4 9.8 %collective-permute-start.2 = (f32[16,1,512]{2,1,0:T(1,128)S(1)}, f32[16,1,512]{2,1,0:T(1,128)S(1)}, u32[]{:S(2)}, u32[]{:S(2)}) collective-permute-start(f32[16,1,512]{2,1,0:T(1,128)S(1)} %get-tuple-element.27), channel_id=1, source_target_pairs={{0,1},{1,2},{2,3},{3,4},{4,5},{5,6},{6,7},{7,8},{8,9},{9,10},{10,1... | collective-permute-start | bytes 98312 | tf_op jit(solution)/shard_map/ppermute | solution.py:18
  32.4 14.4 %collective-permute-start.5 = (f32[1,64,512]{2,1,0:T(8,128)S(1)}, f32[1,64,512]{2,1,0:T(8,128)S(1)}, u32[]{:S(2)}, u32[]{:S(2)}) collective-permute-start(f32[1,64,512]{2,1,0:T(8,128)S(1)} %get-tuple-element.19), channel_id=1, source_target_pairs={{16,0},{32,16},{48,32},{64,48},{80,64},{96,80},{112,96},{128,112},... | collective-permute-start | bytes 393224 | tf_op jit(solution)/shard_map/ppermute | solution.py:19
  34.4 12.4 %collective-permute-start.4 = (f32[1,64,512]{2,1,0:T(8,128)S(1)}, f32[1,64,512]{2,1,0:T(8,128)S(1)}, u32[]{:S(2)}, u32[]{:S(2)}) collective-permute-start(f32[1,64,512]{2,1,0:T(8,128)S(1)} %get-tuple-element.18), channel_id=1, source_target_pairs={{0,16},{16,32},{32,48},{48,64},{64,80},{80,96},{96,112},{112,128},... | collective-permute-start | bytes 393224 | tf_op jit(solution)/shard_map/ppermute | solution.py:18
  38.4 7.4 %collective-permute-start.7 = (f32[16,1,512]{2,1,0:T(1,128)S(1)}, f32[16,1,512]{2,1,0:T(1,128)S(1)}, u32[]{:S(2)}, u32[]{:S(2)}) collective-permute-start(f32[16,1,512]{2,1,0:T(1,128)S(1)} %get-tuple-element.21), channel_id=1, source_target_pairs={{1,0},{2,1},{3,2},{4,3},{5,4},{6,5},{7,6},{8,7},{9,8},{10,9},{11,1... | collective-permute-start | bytes 98312 | tf_op jit(solution)/shard_map/ppermute | solution.py:19
  40.3 6.5 %collective-permute-start.6 = (f32[16,1,512]{2,1,0:T(1,128)S(1)}, f32[16,1,512]{2,1,0:T(1,128)S(1)}, u32[]{:S(2)}, u32[]{:S(2)}) collective-permute-start(f32[16,1,512]{2,1,0:T(1,128)S(1)} %get-tuple-element.20), channel_id=1, source_target_pairs={{0,1},{1,2},{2,3},{3,4},{4,5},{5,6},{6,7},{7,8},{8,9},{9,10},{10,1... | collective-permute-start | bytes 98312 | tf_op jit(solution)/shard_map/ppermute | solution.py:18
  49.8 17.6 %copy-start.6 = (f32[1,16,64,512]{3,2,1,0:T(8,128)S(1)}, f32[1,16,64,512]{3,2,1,0:T(8,128)}, u32[]{:S(2)}) copy-start(f32[1,16,64,512]{3,2,1,0:T(8,128)} %get-tuple-element.23) | copy-start | bytes 6291460
  49.8 17.6 %copy-start.7 = (f32[16,64,512]{2,1,0:T(8,128)S(1)}, f32[16,64,512]{2,1,0:T(8,128)}, u32[]{:S(2)}) copy-start(f32[16,64,512]{2,1,0:T(8,128)} %get-tuple-element.24) | copy-start | bytes 6291460
  49.8 17.6 %copy-start.8 = (f32[1,16,64,512]{3,2,1,0:T(8,128)S(1)}, f32[1,16,64,512]{3,2,1,0:T(8,128)}, u32[]{:S(2)}) copy-start(f32[1,16,64,512]{3,2,1,0:T(8,128)} %get-tuple-element.25) | copy-start | bytes 6291460
  49.9 17.6 %copy-start.9 = (f32[1,16,64,512]{3,2,1,0:T(8,128)S(1)}, f32[1,16,64,512]{3,2,1,0:T(8,128)}, u32[]{:S(2)}) copy-start(f32[1,16,64,512]{3,2,1,0:T(8,128)} %get-tuple-element.26) | copy-start | bytes 6291460
  53.5 15.1 %collective-permute-start.11 = (f32[16,1,512]{2,1,0:T(1,128)S(1)}, f32[16,1,512]{2,1,0:T(1,128)S(1)}, u32[]{:S(2)}, u32[]{:S(2)}) collective-permute-start(f32[16,1,512]{2,1,0:T(1,128)S(1)} %get-tuple-element.17), channel_id=1, source_target_pairs={{1,0},{2,1},{3,2},{4,3},{5,4},{6,5},{7,6},{8,7},{9,8},{10,9},{11,1... | collective-permute-start | bytes 98312 | tf_op jit(solution)/shard_map/ppermute | solution.py:19
  55.4 13.2 %collective-permute-start.10 = (f32[16,1,512]{2,1,0:T(1,128)S(1)}, f32[16,1,512]{2,1,0:T(1,128)S(1)}, u32[]{:S(2)}, u32[]{:S(2)}) collective-permute-start(f32[16,1,512]{2,1,0:T(1,128)S(1)} %get-tuple-element.16), channel_id=1, source_target_pairs={{0,1},{1,2},{2,3},{3,4},{4,5},{5,6},{6,7},{7,8},{8,9},{9,10},{10,1... | collective-permute-start | bytes 98312 | tf_op jit(solution)/shard_map/ppermute | solution.py:18
  61.1 7.5 %collective-permute-start.9 = (f32[1,64,512]{2,1,0:T(8,128)S(1)}, f32[1,64,512]{2,1,0:T(8,128)S(1)}, u32[]{:S(2)}, u32[]{:S(2)}) collective-permute-start(f32[1,64,512]{2,1,0:T(8,128)S(1)} %get-tuple-element.15), channel_id=1, source_target_pairs={{16,0},{32,16},{48,32},{64,48},{80,64},{96,80},{112,96},{128,112},... | collective-permute-start | bytes 393224 | tf_op jit(solution)/shard_map/ppermute | solution.py:19
  63.3 5.9 %collective-permute-start.8 = (f32[1,64,512]{2,1,0:T(8,128)S(1)}, f32[1,64,512]{2,1,0:T(8,128)S(1)}, u32[]{:S(2)}, u32[]{:S(2)}) collective-permute-start(f32[1,64,512]{2,1,0:T(8,128)S(1)} %get-tuple-element.14), channel_id=1, source_target_pairs={{0,16},{16,32},{32,48},{48,64},{64,80},{80,96},{96,112},{112,128},... | collective-permute-start | bytes 393224 | tf_op jit(solution)/shard_map/ppermute | solution.py:18
  76.4 31.3 %collective-permute-start.13 = (f32[1,64,512]{2,1,0:T(8,128)}, f32[1,64,512]{2,1,0:T(8,128)S(1)}, u32[]{:S(2)}, u32[]{:S(2)}) collective-permute-start(f32[1,64,512]{2,1,0:T(8,128)} %get-tuple-element.11), channel_id=1, source_target_pairs={{16,0},{32,16},{48,32},{64,48},{80,64},{96,80},{112,96},{128,112},... | collective-permute-start | bytes 393224 | tf_op jit(solution)/shard_map/ppermute | solution.py:19
  78.3 29.4 %collective-permute-start.12 = (f32[1,64,512]{2,1,0:T(8,128)S(1)}, f32[1,64,512]{2,1,0:T(8,128)S(1)}, u32[]{:S(2)}, u32[]{:S(2)}) collective-permute-start(f32[1,64,512]{2,1,0:T(8,128)S(1)} %get-tuple-element.10), channel_id=1, source_target_pairs={{0,16},{16,32},{32,48},{48,64},{64,80},{80,96},{96,112},{112,128},... | collective-permute-start | bytes 393224 | tf_op jit(solution)/shard_map/ppermute | solution.py:18
  83.4 22.7 %collective-permute-start.15 = (f32[16,1,512]{2,1,0:T(1,128)}, f32[16,1,512]{2,1,0:T(1,128)}, u32[]{:S(2)}, u32[]{:S(2)}) collective-permute-start(f32[16,1,512]{2,1,0:T(1,128)} %get-tuple-element.13), channel_id=1, source_target_pairs={{1,0},{2,1},{3,2},{4,3},{5,4},{6,5},{7,6},{8,7},{9,8},{10,9},{11,1... | collective-permute-start | bytes 98312 | tf_op jit(solution)/shard_map/ppermute | solution.py:19
  85.3 21.6 %collective-permute-start.14 = (f32[16,1,512]{2,1,0:T(1,128)}, f32[16,1,512]{2,1,0:T(1,128)}, u32[]{:S(2)}, u32[]{:S(2)}) collective-permute-start(f32[16,1,512]{2,1,0:T(1,128)} %get-tuple-element.12), channel_id=1, source_target_pairs={{0,1},{1,2},{2,3},{3,4},{4,5},{5,6},{6,7},{7,8},{8,9},{9,10},{10,1... | collective-permute-start | bytes 98312 | tf_op jit(solution)/shard_map/ppermute | solution.py:18
  91.6 16.1 %copy-start.2 = (f32[16,64,512]{2,1,0:T(8,128)S(1)}, f32[16,64,512]{2,1,0:T(8,128)}, u32[]{:S(2)}) copy-start(f32[16,64,512]{2,1,0:T(8,128)} %copy-done.1) | copy-start | bytes 6291460
  95.0 28.4 %all-to-all-start = ((f32[16,1,8192]{2,1,0:T(1,128)}), f32[16,1,8192]{2,1,0:T(1,128)S(1)}, u32[]{:S(2)}, u32[]{:S(2)}) async-start(f32[16,1,8192]{2,1,0:T(1,128)} %reshape.111), calls=%async_computation | async-start | bytes 1048576 | tf_op jit(solution)/shard_map/all_to_all | solution.py:72
  123.4 23.4 %all-to-all-start.1 = ((f32[16,1,8192]{2,1,0:T(1,128)}), f32[16,1,8192]{2,1,0:T(1,128)S(1)}, u32[]{:S(2)}, u32[]{:S(2)}) async-start(f32[16,1,8192]{2,1,0:T(1,128)} %reshape.113), calls=%async_computation.1 | async-start | bytes 1048576 | tf_op jit(solution)/shard_map/all_to_all | solution.py:72
  (8 other events, 26.8 us)
where the time goes:
time: 152 us; the launch traced here: 151 us
  starting transfers between devices  71.7 us (47%)
  other arithmetic  42.2 us (28%)
  local copies, waits for them, and re-layouts  19.6 us (13%)
  waiting for transfers between devices  15.1 us (10%)
  between operations  2.04 us (1%)
    ppermute x8, starting transfers between devices, padded_2(): lax.ppermute(last, axis, up)  38.6 us
    all_to_all x2, starting transfers between devices, composite(): lax.all_to_all(packed, 'depth', split_axis=3, concat_axis=0, tiled=True)  17.1 us
    ppermute x8, starting transfers between devices, padded_2(): lax.ppermute(leading, axis, [(b, a) for a, b in up])  16 us
    sub x3, other arithmetic, update(): return center - step_size * rate  13.7 us
    all_to_all x2, waiting for transfers between devices, composite(): lax.all_to_all(packed, 'depth', split_axis=3, concat_axis=0, tiled=True)  13.6 us
    concatenate x4, other arithmetic, padded_2(): jnp.concatenate([jnp.pad(low, around), array, jnp.pad(high, around)], axi...  10.3 us
    unnamed x34, local copies, waits for them, and re-layouts  9.96 us
    another operation x1, other arithmetic, render_brick(): jnp.stack([jax.nn.sigmoid(2.0 * field), jnp.exp(-field * field), jax.nn.s...  5.46 us
  transfers between devices with their start and end apart: 18, of which 4 were waited for; matrix products, arithmetic and copies ran while one was open for 21% of the time, Pallas kernels for 0%

commit v1 on v0

--- a/solution.py
+++ b/solution.py
@@ -69,7 +69,10 @@
     rows, cols = (logs.shape[1], logs.shape[2])
     width = cols // depth_count
     packed = jnp.concatenate([colours, logs[:, None]], axis=1)
-    received = lax.all_to_all(packed, "depth", split_axis=3, concat_axis=0, tiled=True)
+    received = jnp.concatenate(
+        lax.all_to_all(jnp.stack(jnp.split(packed, lax.axis_size("depth"), axis=3)), "depth", 0, 0),
+        axis=0,
+    )
     received = received.reshape(depth_count, count, 4, rows, width)
     earlier_mask = (slab_rank[None, :] < slab_rank[:, None]).astype(jnp.float32)
     log_parts = received[:, :, 3]

time: 152 us -> 171 us (1.12)
  other arithmetic: 42.2 us -> 57.9 us
  waiting for transfers between devices: 15.1 us -> 20 us
  starting transfers between devices: 71.7 us -> 69.9 us
    unnamed x1 -> x31, other arithmetic: 0.01 us -> 12.1 us
    ppermute x8, starting transfers between devices: 38.6 us -> 29.6 us  [padded_2(): lax.ppermute(last, axis, up)]
    ppermute x8, waiting for transfers between devices: 0.02 us -> 6.48 us  [padded_2(): lax.ppermute(leading, axis, [(b, a) for a, b in up])]
    all_to_all x2, starting transfers between devices: 17.1 us -> 21.2 us  [composite(): lax.all_to_all(jnp.stack(jnp.split(packed, lax.axis_size('depth'), axis=3...]
    ppermute x8, starting transfers between devices: 16 us -> 19 us  [padded_2(): lax.ppermute(leading, axis, [(b, a) for a, b in up])]
    reduce_sum x2, other arithmetic: 2.17 us -> 5.06 us  [render_brick(): partial_colour = jnp.sum(weight[None] * colour, axis=1)]
    another operation x0 -> x2, local copies, waits for them, and re-layouts: none -> 2.77 us  [composite(): jnp.stack(jnp.split(packed, lax.axis_size('depth'), axis=3))]
    concatenate x2 -> x0, local copies, waits for them, and re-layouts: 1.97 us -> none  [composite(): packed = jnp.concatenate([colours, logs[:, None]], axis=1)]
  transfers between devices with their start and end apart: 18 -> 18, of which waited for: 4 -> 4; matrix products, arithmetic and copies ran while one was open for 21% -> 20% of each run, Pallas kernels for 0% -> 0%
where the time goes in v1:
time: 171 us; the launch traced here: 169 us
  starting transfers between devices  69.9 us (41%)
  other arithmetic  57.9 us (34%)
  waiting for transfers between devices  20 us (12%)
  local copies, waits for them, and re-layouts  18.3 us (11%)
  between operations  2.05 us (1%)
    ppermute x8, starting transfers between devices, padded_2(): lax.ppermute(last, axis, up)  29.6 us
    all_to_all x2, starting transfers between devices, composite(): lax.all_to_all(jnp.stack(jnp.split(packed, lax.axis_size('depth'), axis=3...  21.2 us
    ppermute x8, starting transfers between devices, padded_2(): lax.ppermute(leading, axis, [(b, a) for a, b in up])  19 us
    sub x3, other arithmetic, update(): return center - step_size * rate  13.6 us
    all_to_all x2, waiting for transfers between devices, composite(): lax.all_to_all(jnp.stack(jnp.split(packed, lax.axis_size('depth'), axis=3...  13.5 us
    unnamed x31, other arithmetic  12.1 us
    concatenate x4, other arithmetic, padded_2(): jnp.concatenate([jnp.pad(low, around), array, jnp.pad(high, around)], axi...  10.3 us
    unnamed x26, local copies, waits for them, and re-layouts  8.91 us
  transfers between devices with their start and end apart: 18, of which 4 were waited for; matrix products, arithmetic and copies ran while one was open for 20% of the time, Pallas kernels for 0%

profile of v1, /device:TPU:27, one launch (start us, length us, event | category | flops | bytes accessed | tf_op | source)
XLA Modules:
  0.0 169.0 jit_solution(9684758625917184334)
XLA Ops:
  1.6 4.1 %collective-permute-start = (f32[1,64,512]{2,1,0:T(8,128)S(1)}, f32[1,64,512]{2,1,0:T(8,128)S(1)}, u32[]{:S(2)}, u32[]{:S(2)}) collective-permute-start(f32[1,64,512]{2,1,0:T(8,128)S(1)} %get-tuple-element.30), channel_id=1, source_target_pairs={{0,16},{16,32},{32,48},{48,64},{64,80},{80,96},{96,112},{112,128},... | collective-permute-start | bytes 393224 | tf_op jit(solution)/shard_map/ppermute | solution.py:18
  8.8 2.8 %collective-permute-start.2 = (f32[16,1,512]{2,1,0:T(1,128)S(1)}, f32[16,1,512]{2,1,0:T(1,128)S(1)}, u32[]{:S(2)}, u32[]{:S(2)}) collective-permute-start(f32[16,1,512]{2,1,0:T(1,128)S(1)} %get-tuple-element.27), channel_id=1, source_target_pairs={{0,1},{1,2},{2,3},{3,4},{4,5},{5,6},{6,7},{7,8},{8,9},{9,10},{10,1... | collective-permute-start | bytes 98312 | tf_op jit(solution)/shard_map/ppermute | solution.py:18
  11.5 2.5 %collective-permute-start.3 = (f32[16,1,512]{2,1,0:T(1,128)S(1)}, f32[16,1,512]{2,1,0:T(1,128)S(1)}, u32[]{:S(2)}, u32[]{:S(2)}) collective-permute-start(f32[16,1,512]{2,1,0:T(1,128)S(1)} %get-tuple-element.28), channel_id=1, source_target_pairs={{1,0},{2,1},{3,2},{4,3},{5,4},{6,5},{7,6},{8,7},{9,8},{10,9},{11,1... | collective-permute-start | bytes 98312 | tf_op jit(solution)/shard_map/ppermute | solution.py:19
  23.4 6.7 %fusion.59 = (f32[16,64,512]{2,1,0:T(8,128)S(1)}, f32[1,16,64,512]{3,2,1,0:T(8,128)}, f32[16,64,512]{2,1,0:T(8,128)}, f32[1,16,64,512]{3,2,1,0:T(8,128)}, f32[1,16,64,512]{3,2,1,0:T(8,128)}) fusion(f32[16,64,512]{2,1,0:T(8,128)S(1)} %copy-done, f32[18,66,514]{2,1,0:T(8,128)S(1)} %select_maximum_fusion.12, f32[18,1,512]{2,1,0:T(1,128)S(1)} %pad.39, ...), kind=kLoop, calls=%fused_computation.140 | loop fusion | flops 24641536 | bytes 27992064 | tf_op jit(solution)/shard_map/sub | solution.py:42
  30.2 4.0 %fusion = f32[3,64,512]{2,1,0:T(8,128)S(1)} fusion(f32[1,16,64,512]{3,2,1,0:T(8,128)} %get-tuple-element.25, f32[1,16,64,512]{3,2,1,0:T(8,128)} %get-tuple-element.23, f32[1,16,64,512]{3,2,1,0:T(8,128)} %get-tuple-element.26, f32[16,64,512]{2,1,0:T(8,128)} %get-tuple-element.24), kind=kLoop, calls=%fused_computation.1 | loop fusion | flops 6193152 | bytes 8781824 | tf_op jit(solution)/shard_map/reduce_sum | solution.py:60
  43.0 4.5 %collective-permute-start.4 = (f32[1,64,512]{2,1,0:T(8,128)S(1)}, f32[1,64,512]{2,1,0:T(8,128)S(1)}, u32[]{:S(2)}, u32[]{:S(2)}) collective-permute-start(f32[1,64,512]{2,1,0:T(8,128)S(1)} %get-tuple-element.18), channel_id=1, source_target_pairs={{0,16},{16,32},{32,48},{48,64},{64,80},{80,96},{96,112},{112,128},... | collective-permute-start | bytes 393224 | tf_op jit(solution)/shard_map/ppermute | solution.py:18
  50.1 4.6 %collective-permute-start.6 = (f32[16,1,512]{2,1,0:T(1,128)S(1)}, f32[16,1,512]{2,1,0:T(1,128)S(1)}, u32[]{:S(2)}, u32[]{:S(2)}) collective-permute-start(f32[16,1,512]{2,1,0:T(1,128)S(1)} %get-tuple-element.20), channel_id=1, source_target_pairs={{0,1},{1,2},{2,3},{3,4},{4,5},{5,6},{6,7},{7,8},{8,9},{9,10},{10,1... | collective-permute-start | bytes 98312 | tf_op jit(solution)/shard_map/ppermute | solution.py:18
  57.4 4.0 %collective-permute-done.7 = f32[16,1,512]{2,1,0:T(1,128)S(1)} collective-permute-done((f32[16,1,512]{2,1,0:T(1,128)S(1)}, f32[16,1,512]{2,1,0:T(1,128)S(1)}, u32[]{:S(2)}, u32[]{:S(2)}) %collective-permute-start.7) | collective-permute-done | bytes 32800 | tf_op jit(solution)/shard_map/ppermute | solution.py:19
  61.5 3.0 %select_maximum_fusion.8 = f32[18,66,514]{2,1,0:T(8,128)S(1)} fusion(f32[18,1,512]{2,1,0:T(1,128)S(1)} %pad.42, f32[18,1,512]{2,1,0:T(1,128)S(1)} %pad.41, f32[1,64,512]{2,1,0:T(8,128)S(1)} %collective-permute-done.5, f32[16,64,512]{2,1,0:T(8,128)S(1)} %get-tuple-element.22, f32[1,64,512]{2,1,0:T(8,128)S(1)} %collective-permute-done.4), kind=kLoop, calls=%fused_computation.14 | loop fusion | flops 7327584 | bytes 4875552 | tf_op jit(solution)/shard_map/concatenate | solution.py:25
  64.5 3.4 %fusion.42 = f32[16,64,512]{2,1,0:T(8,128)S(1)} fusion(f32[16,64,512]{2,1,0:T(8,128)S(1)} %get-tuple-element.22, f32[18,66,514]{2,1,0:T(8,128)S(1)} %select_maximum_fusion.8, f32[18,1,512]{2,1,0:T(1,128)S(1)} %pad.42, f32[1,64,512]{2,1,0:T(8,128)S(1)} %collective-permute-done.5, f32[1,64,512]{2,1,0:T(8,128)S(1)} %collective-permute-done.4, ...), kind=kLoop, calls=%fused_computation.113 | loop fusion | flops 17301504 | bytes 15015936 | tf_op jit(solution)/shard_map/sub | solution.py:42
  67.9 5.1 %collective-permute-start.8 = (f32[1,64,512]{2,1,0:T(8,128)S(1)}, f32[1,64,512]{2,1,0:T(8,128)S(1)}, u32[]{:S(2)}, u32[]{:S(2)}) collective-permute-start(f32[1,64,512]{2,1,0:T(8,128)S(1)} %get-tuple-element.14), channel_id=1, source_target_pairs={{0,16},{16,32},{32,48},{48,64},{64,80},{80,96},{96,112},{112,128},... | collective-permute-start | bytes 393224 | tf_op jit(solution)/shard_map/ppermute | solution.py:18
  76.9 3.5 %collective-permute-start.11 = (f32[16,1,512]{2,1,0:T(1,128)S(1)}, f32[16,1,512]{2,1,0:T(1,128)S(1)}, u32[]{:S(2)}, u32[]{:S(2)}) collective-permute-start(f32[16,1,512]{2,1,0:T(1,128)S(1)} %get-tuple-element.17), channel_id=1, source_target_pairs={{1,0},{2,1},{3,2},{4,3},{5,4},{6,5},{7,6},{8,7},{9,8},{10,9},{11,1... | collective-permute-start | bytes 98312 | tf_op jit(solution)/shard_map/ppermute | solution.py:19
  81.2 2.4 %collective-permute-done.11 = f32[16,1,512]{2,1,0:T(1,128)S(1)} collective-permute-done((f32[16,1,512]{2,1,0:T(1,128)S(1)}, f32[16,1,512]{2,1,0:T(1,128)S(1)}, u32[]{:S(2)}, u32[]{:S(2)}) %collective-permute-start.11) | collective-permute-done | bytes 32800 | tf_op jit(solution)/shard_map/ppermute | solution.py:19
  83.7 3.0 %select_maximum_fusion.4 = f32[18,66,514]{2,1,0:T(8,128)S(1)} fusion(f32[18,1,512]{2,1,0:T(1,128)S(1)} %pad.45, f32[18,1,512]{2,1,0:T(1,128)S(1)} %pad.44, f32[1,64,512]{2,1,0:T(8,128)S(1)} %collective-permute-done.9, f32[16,64,512]{2,1,0:T(8,128)S(1)} %fusion.42, f32[1,64,512]{2,1,0:T(8,128)S(1)} %collective-permute-done.8), kind=kLoop, calls=%fused_computation.10 | loop fusion | flops 7327584 | bytes 4875552 | tf_op jit(solution)/shard_map/concatenate | solution.py:25
  86.7 3.5 %fusion.25 = f32[16,64,512]{2,1,0:T(8,128)S(1)} fusion(f32[16,64,512]{2,1,0:T(8,128)S(1)} %fusion.42, f32[18,66,514]{2,1,0:T(8,128)S(1)} %select_maximum_fusion.4, f32[18,1,512]{2,1,0:T(1,128)S(1)} %pad.45, f32[1,64,512]{2,1,0:T(8,128)S(1)} %collective-permute-done.9, f32[1,64,512]{2,1,0:T(8,128)S(1)} %collective-permute-done.8, f32[18,1,512]{2,1,0:T(1,128)S(1)} %pad.44, ...), kind=kLoop, calls=%fused_computation.86 | loop fusion | flops 17301504 | bytes 15015936 | tf_op jit(solution)/shard_map/sub | solution.py:42
  91.0 4.8 %collective-permute-start.12 = (f32[1,64,512]{2,1,0:T(8,128)}, f32[1,64,512]{2,1,0:T(8,128)S(1)}, u32[]{:S(2)}, u32[]{:S(2)}) collective-permute-start(f32[1,64,512]{2,1,0:T(8,128)} %get-tuple-element.10), channel_id=1, source_target_pairs={{0,16},{16,32},{32,48},{48,64},{64,80},{80,96},{96,112},{112,128},... | collective-permute-start | bytes 393224 | tf_op jit(solution)/shard_map/ppermute | solution.py:18
  100.3 3.4 %collective-permute-start.15 = (f32[16,1,512]{2,1,0:T(1,128)}, f32[16,1,512]{2,1,0:T(1,128)}, u32[]{:S(2)}, u32[]{:S(2)}) collective-permute-start(f32[16,1,512]{2,1,0:T(1,128)} %get-tuple-element.13), channel_id=1, source_target_pairs={{1,0},{2,1},{3,2},{4,3},{5,4},{6,5},{7,6},{8,7},{9,8},{10,9},{11,1... | collective-permute-start | bytes 98312 | tf_op jit(solution)/shard_map/ppermute | solution.py:19
  104.4 2.2 %copy.41 = f32[16,1,4,64,32]{3,4,2,1,0:T(8,128)S(1)} copy(f32[16,1,4,64,32]{4,3,2,1,0:T(8,128)} %fusion.178) | data formatting | bytes 1048576 | tf_op jit(solution)/shard_map/stack | solution.py:73
  108.1 14.1 %all-to-all-start = ((f32[16,1,8192]{2,1,0:T(1,128)}), f32[16,1,8192]{2,1,0:T(1,128)}, u32[]{:S(2)}, u32[]{:S(2)}) async-start(f32[16,1,8192]{2,1,0:T(1,128)} %reshape.107), calls=%async_computation | async-start | bytes 1048576 | tf_op jit(solution)/shard_map/all_to_all | solution.py:73
  123.8 3.0 %select_maximum_fusion = f32[18,66,514]{2,1,0:T(8,128)S(1)} fusion(f32[18,1,512]{2,1,0:T(1,128)S(1)} %pad.48, f32[18,1,512]{2,1,0:T(1,128)S(1)} %pad.47, f32[1,64,512]{2,1,0:T(8,128)S(1)} %collective-permute-done.13, f32[16,64,512]{2,1,0:T(8,128)S(1)} %copy-done.2, f32[1,64,512]{2,1,0:T(8,128)S(1)} %collective-permute-done.12), kind=kLoop, calls=%fused_computation.6 | loop fusion | flops 7327584 | bytes 4875552 | tf_op jit(solution)/shard_map/concatenate | solution.py:25
  126.8 5.5 %divide_bitcast_fusion.1 = (f32[1,16,64,512]{3,2,1,0:T(8,128)S(1)}, f32[16,64,512]{2,1,0:T(8,128)S(1)}) fusion(f32[16,64,512]{2,1,0:T(8,128)S(1)} %copy-done.2, f32[18,66,514]{2,1,0:T(8,128)S(1)} %select_maximum_fusion, f32[3,16,64,512]{3,2,1,0:T(8,128)} %param.5, f32[18,1,512]{2,1,0:T(1,128)S(1)} %pad.48, f32[1,64,512]{2,1,0:T(8,128)S(1)} %collective-permute-done.13, ...), kind=kLoop, calls=%fused_computation.160 | loop fusion | flops 19398656 | bytes 17113088 | tf_op jit(solution)/shard_map/stack | solution.py:53
  139.6 7.1 %all-to-all-start.1 = ((f32[16,1,8192]{2,1,0:T(1,128)}), f32[16,1,8192]{2,1,0:T(1,128)S(1)}, u32[]{:S(2)}, u32[]{:S(2)}) async-start(f32[16,1,8192]{2,1,0:T(1,128)} %reshape.109), calls=%async_computation.1 | async-start | bytes 1048576 | tf_op jit(solution)/shard_map/all_to_all | solution.py:73
  147.2 2.9 %reduce.7 = f32[16,8192]{1,0:T(8,128)S(1)} reduce(f32[16,1,8192]{2,1,0:T(1,128)} %all-to-all-done, f32[]{:T(128)} %broadcast.196), dimensions={1}, to_apply=%all_to_all.6.reduce_sub_computation | reduce | bytes 1048580 | tf_op jit(solution)/shard_map/all_to_all | solution.py:73
  150.6 13.4 %all-to-all-done.1 = f32[16,1,8192]{2,1,0:T(1,128)S(1)} async-done(((f32[16,1,8192]{2,1,0:T(1,128)}), f32[16,1,8192]{2,1,0:T(1,128)S(1)}, u32[]{:S(2)}, u32[]{:S(2)}) %all-to-all-start.1) | async-done | bytes 524320 | tf_op jit(solution)/shard_map/all_to_all | solution.py:73
  (120 shorter events, 53.5 us)
Async XLA Ops:
  1.6 17.3 %collective-permute-start = (f32[1,64,512]{2,1,0:T(8,128)S(1)}, f32[1,64,512]{2,1,0:T(8,128)S(1)}, u32[]{:S(2)}, u32[]{:S(2)}) collective-permute-start(f32[1,64,512]{2,1,0:T(8,128)S(1)} %get-tuple-element.30), channel_id=1, source_target_pairs={{0,16},{16,32},{32,48},{48,64},{64,80},{80,96},{96,112},{112,128},... | collective-permute-start | bytes 393224 | tf_op jit(solution)/shard_map/ppermute | solution.py:18
  5.7 15.2 %collective-permute-start.1 = (f32[1,64,512]{2,1,0:T(8,128)S(1)}, f32[1,64,512]{2,1,0:T(8,128)S(1)}, u32[]{:S(2)}, u32[]{:S(2)}) collective-permute-start(f32[1,64,512]{2,1,0:T(8,128)S(1)} %get-tuple-element.29), channel_id=1, source_target_pairs={{16,0},{32,16},{48,32},{64,48},{80,64},{96,80},{112,96},{128,112},... | collective-permute-start | bytes 393224 | tf_op jit(solution)/shard_map/ppermute | solution.py:19
  8.8 10.1 %collective-permute-start.2 = (f32[16,1,512]{2,1,0:T(1,128)S(1)}, f32[16,1,512]{2,1,0:T(1,128)S(1)}, u32[]{:S(2)}, u32[]{:S(2)}) collective-permute-start(f32[16,1,512]{2,1,0:T(1,128)S(1)} %get-tuple-element.27), channel_id=1, source_target_pairs={{0,1},{1,2},{2,3},{3,4},{4,5},{5,6},{6,7},{7,8},{8,9},{9,10},{10,1... | collective-permute-start | bytes 98312 | tf_op jit(solution)/shard_map/ppermute | solution.py:18
  11.5 6.0 %copy-start.7 = (s32[16]{0:T(128)S(1)}, s32[16]{0:T(128)}, u32[]{:S(2)}) copy-start(s32[16]{0:T(128)} %param.6) | copy-start | bytes 196
  11.5 7.3 %collective-permute-start.3 = (f32[16,1,512]{2,1,0:T(1,128)S(1)}, f32[16,1,512]{2,1,0:T(1,128)S(1)}, u32[]{:S(2)}, u32[]{:S(2)}) collective-permute-start(f32[16,1,512]{2,1,0:T(1,128)S(1)} %get-tuple-element.28), channel_id=1, source_target_pairs={{1,0},{2,1},{3,2},{4,3},{5,4},{6,5},{7,6},{8,7},{9,8},{10,9},{11,1... | collective-permute-start | bytes 98312 | tf_op jit(solution)/shard_map/ppermute | solution.py:19
  14.1 8.2 %slice-start = ((s8[6291456]{0:T(1024)(128)(4,1)}), s8[2097152]{0:T(1024)(128)(4,1)S(1)}, s32[]{:S(2)}) async-start(s8[6291456]{0:T(1024)(128)(4,1)} %bitcast.244), calls=%async_computation.2 | async-start | bytes 4194304
  18.9 3.4 %slice-start.1 = ((s8[6291456]{0:T(1024)(128)(4,1)}), s8[4194304]{0:T(1024)(128)(4,1)S(1)}, s32[]{:S(2)}) async-start(s8[6291456]{0:T(1024)(128)(4,1)} %bitcast.244), calls=%async_computation.3 | async-start | bytes 8388608
  43.0 18.5 %collective-permute-start.4 = (f32[1,64,512]{2,1,0:T(8,128)S(1)}, f32[1,64,512]{2,1,0:T(8,128)S(1)}, u32[]{:S(2)}, u32[]{:S(2)}) collective-permute-start(f32[1,64,512]{2,1,0:T(8,128)S(1)} %get-tuple-element.18), channel_id=1, source_target_pairs={{0,16},{16,32},{32,48},{48,64},{64,80},{80,96},{96,112},{112,128},... | collective-permute-start | bytes 393224 | tf_op jit(solution)/shard_map/ppermute | solution.py:18
  47.5 14.0 %collective-permute-start.5 = (f32[1,64,512]{2,1,0:T(8,128)S(1)}, f32[1,64,512]{2,1,0:T(8,128)S(1)}, u32[]{:S(2)}, u32[]{:S(2)}) collective-permute-start(f32[1,64,512]{2,1,0:T(8,128)S(1)} %get-tuple-element.19), channel_id=1, source_target_pairs={{16,0},{32,16},{48,32},{64,48},{80,64},{96,80},{112,96},{128,112},... | collective-permute-start | bytes 393224 | tf_op jit(solution)/shard_map/ppermute | solution.py:19
  50.1 7.3 %collective-permute-start.6 = (f32[16,1,512]{2,1,0:T(1,128)S(1)}, f32[16,1,512]{2,1,0:T(1,128)S(1)}, u32[]{:S(2)}, u32[]{:S(2)}) collective-permute-start(f32[16,1,512]{2,1,0:T(1,128)S(1)} %get-tuple-element.20), channel_id=1, source_target_pairs={{0,1},{1,2},{2,3},{3,4},{4,5},{5,6},{6,7},{7,8},{8,9},{9,10},{10,1... | collective-permute-start | bytes 98312 | tf_op jit(solution)/shard_map/ppermute | solution.py:18
  54.7 6.8 %collective-permute-start.7 = (f32[16,1,512]{2,1,0:T(1,128)S(1)}, f32[16,1,512]{2,1,0:T(1,128)S(1)}, u32[]{:S(2)}, u32[]{:S(2)}) collective-permute-start(f32[16,1,512]{2,1,0:T(1,128)S(1)} %get-tuple-element.21), channel_id=1, source_target_pairs={{1,0},{2,1},{3,2},{4,3},{5,4},{6,5},{7,6},{8,7},{9,8},{10,9},{11,1... | collective-permute-start | bytes 98312 | tf_op jit(solution)/shard_map/ppermute | solution.py:19
  67.9 15.8 %collective-permute-start.8 = (f32[1,64,512]{2,1,0:T(8,128)S(1)}, f32[1,64,512]{2,1,0:T(8,128)S(1)}, u32[]{:S(2)}, u32[]{:S(2)}) collective-permute-start(f32[1,64,512]{2,1,0:T(8,128)S(1)} %get-tuple-element.14), channel_id=1, source_target_pairs={{0,16},{16,32},{32,48},{48,64},{64,80},{80,96},{96,112},{112,128},... | collective-permute-start | bytes 393224 | tf_op jit(solution)/shard_map/ppermute | solution.py:18
  73.0 10.7 %collective-permute-start.9 = (f32[1,64,512]{2,1,0:T(8,128)S(1)}, f32[1,64,512]{2,1,0:T(8,128)S(1)}, u32[]{:S(2)}, u32[]{:S(2)}) collective-permute-start(f32[1,64,512]{2,1,0:T(8,128)S(1)} %get-tuple-element.15), channel_id=1, source_target_pairs={{16,0},{32,16},{48,32},{64,48},{80,64},{96,80},{112,96},{128,112},... | collective-permute-start | bytes 393224 | tf_op jit(solution)/shard_map/ppermute | solution.py:19
  74.9 6.3 %collective-permute-start.10 = (f32[16,1,512]{2,1,0:T(1,128)S(1)}, f32[16,1,512]{2,1,0:T(1,128)S(1)}, u32[]{:S(2)}, u32[]{:S(2)}) collective-permute-start(f32[16,1,512]{2,1,0:T(1,128)S(1)} %get-tuple-element.16), channel_id=1, source_target_pairs={{0,1},{1,2},{2,3},{3,4},{4,5},{5,6},{6,7},{7,8},{8,9},{9,10},{10,1... | collective-permute-start | bytes 98312 | tf_op jit(solution)/shard_map/ppermute | solution.py:18
  76.9 6.8 %collective-permute-start.11 = (f32[16,1,512]{2,1,0:T(1,128)S(1)}, f32[16,1,512]{2,1,0:T(1,128)S(1)}, u32[]{:S(2)}, u32[]{:S(2)}) collective-permute-start(f32[16,1,512]{2,1,0:T(1,128)S(1)} %get-tuple-element.17), channel_id=1, source_target_pairs={{1,0},{2,1},{3,2},{4,3},{5,4},{6,5},{7,6},{8,7},{9,8},{10,9},{11,1... | collective-permute-start | bytes 98312 | tf_op jit(solution)/shard_map/ppermute | solution.py:19
  90.2 7.5 %copy-start.1 = (f32[16,64,512]{2,1,0:T(8,128)}, f32[16,64,512]{2,1,0:T(8,128)S(1)}, u32[]{:S(2)}) copy-start(f32[16,64,512]{2,1,0:T(8,128)S(1)} %fusion.25) | copy-start | bytes 6291460
  91.0 32.8 %collective-permute-start.12 = (f32[1,64,512]{2,1,0:T(8,128)}, f32[1,64,512]{2,1,0:T(8,128)S(1)}, u32[]{:S(2)}, u32[]{:S(2)}) collective-permute-start(f32[1,64,512]{2,1,0:T(8,128)} %get-tuple-element.10), channel_id=1, source_target_pairs={{0,16},{16,32},{32,48},{48,64},{64,80},{80,96},{96,112},{112,128},... | collective-permute-start | bytes 393224 | tf_op jit(solution)/shard_map/ppermute | solution.py:18
  95.7 28.0 %collective-permute-start.13 = (f32[1,64,512]{2,1,0:T(8,128)S(1)}, f32[1,64,512]{2,1,0:T(8,128)S(1)}, u32[]{:S(2)}, u32[]{:S(2)}) collective-permute-start(f32[1,64,512]{2,1,0:T(8,128)S(1)} %get-tuple-element.11), channel_id=1, source_target_pairs={{16,0},{32,16},{48,32},{64,48},{80,64},{96,80},{112,96},{128,112},... | collective-permute-start | bytes 393224 | tf_op jit(solution)/shard_map/ppermute | solution.py:19
  98.4 23.8 %collective-permute-start.14 = (f32[16,1,512]{2,1,0:T(1,128)}, f32[16,1,512]{2,1,0:T(1,128)}, u32[]{:S(2)}, u32[]{:S(2)}) collective-permute-start(f32[16,1,512]{2,1,0:T(1,128)} %get-tuple-element.12), channel_id=1, source_target_pairs={{0,1},{1,2},{2,3},{3,4},{4,5},{5,6},{6,7},{7,8},{8,9},{9,10},{10,1... | collective-permute-start | bytes 98312 | tf_op jit(solution)/shard_map/ppermute | solution.py:18
  100.3 22.7 %collective-permute-start.15 = (f32[16,1,512]{2,1,0:T(1,128)}, f32[16,1,512]{2,1,0:T(1,128)}, u32[]{:S(2)}, u32[]{:S(2)}) collective-permute-start(f32[16,1,512]{2,1,0:T(1,128)} %get-tuple-element.13), channel_id=1, source_target_pairs={{1,0},{2,1},{3,2},{4,3},{5,4},{6,5},{7,6},{8,7},{9,8},{10,9},{11,1... | collective-permute-start | bytes 98312 | tf_op jit(solution)/shard_map/ppermute | solution.py:19
  106.6 17.2 %copy-start.2 = (f32[16,64,512]{2,1,0:T(8,128)S(1)}, f32[16,64,512]{2,1,0:T(8,128)}, u32[]{:S(2)}) copy-start(f32[16,64,512]{2,1,0:T(8,128)} %copy-done.1) | copy-start | bytes 6291460
  108.1 31.5 %all-to-all-start = ((f32[16,1,8192]{2,1,0:T(1,128)}), f32[16,1,8192]{2,1,0:T(1,128)}, u32[]{:S(2)}, u32[]{:S(2)}) async-start(f32[16,1,8192]{2,1,0:T(1,128)} %reshape.107), calls=%async_computation | async-start | bytes 1048576 | tf_op jit(solution)/shard_map/all_to_all | solution.py:73
  139.6 24.5 %all-to-all-start.1 = ((f32[16,1,8192]{2,1,0:T(1,128)}), f32[16,1,8192]{2,1,0:T(1,128)S(1)}, u32[]{:S(2)}, u32[]{:S(2)}) async-start(f32[16,1,8192]{2,1,0:T(1,128)} %reshape.109), calls=%async_computation.1 | async-start | bytes 1048576 | tf_op jit(solution)/shard_map/all_to_all | solution.py:73
  150.6 15.8 %copy-start.6 = (s32[16]{0:T(128)S(1)}, s32[16]{0:T(128)}, u32[]{:S(2)}) copy-start(s32[16]{0:T(128)} %param.7) | copy-start | bytes 196
  (4 other events, 6.8 us)
